TPU v7x, 32 devices: a whole 2x2x4 slice. The times are simulated.
32 devices in a mesh: grp: 1, src: 16 (over z, y, x), srf: 2 (over core).
Axes of the slice: x: 2, y: 2, z: 4, core: 2. Of those that a mesh axis runs over, the one named last changes fastest.
Arguments:
- left_traces: bfloat16 [128, 512, 256], P(('grp', 'src'), 'srf'), may hold values from -6 to 6
- right_traces: bfloat16 [2, 256, 512, 256], P('srf', 'src', 'grp'), may hold values from -0.03125 to 0.03125
- surf_map: int32 [512], P(('grp', 'srf')), may hold values from 0 to 255, as said below
- shot_map: int32 [512], P(('grp', 'srf')), may hold values from 0 to 255, as said below
Outputs:
- multiples: bfloat16 [128, 512, 256], P(('grp', 'src'), 'srf')
Inputs may be any that keep to these rules, and one draw needn't show every extreme that they name: `surf_map`: each aligned block of 256 entries holds every number of 0 to 255 once. `shot_map`: each aligned block of 256 entries holds every number of 0 to 255 once.
All inputs are finite; a program needn't handle non-finite values.
Results may differ from a plain program's by a relative error of at most 0.0058.
Values may be sent and summed in bfloat16 or wider, within the bound.
A program may use at most 192 MiB of HBM per device.

v0:
```python
import math

import jax
import jax.numpy as jnp
from jax import lax
from jax.sharding import PartitionSpec as P

BINS = 40


FULL_ACCURACY = lax.Precision.HIGHEST


def tables(samples, bin_count):
    bin_index = jnp.arange(1, bin_count + 1, dtype=jnp.int32)
    time_index = jnp.arange(samples, dtype=jnp.int32)
    phase_int = bin_index[:, None] * time_index[None, :] % samples
    angles = phase_int.astype(jnp.float32) * (2.0 * math.pi / samples)
    forward = jnp.concatenate([jnp.cos(angles), -jnp.sin(angles)], axis=0)
    inverse = forward * (2.0 / samples)
    return (forward, inverse)


def complex_product(left_operand, right_operand):
    real_component = jnp.einsum(
        "evz,ezh->evh", left_operand[0], right_operand[0], preferred_element_type=jnp.float32
    ) - jnp.einsum(
        "evz,ezh->evh", left_operand[1], right_operand[1], preferred_element_type=jnp.float32
    )
    imaginary_component = jnp.einsum(
        "evz,ezh->evh", left_operand[0], right_operand[1], preferred_element_type=jnp.float32
    ) + jnp.einsum(
        "evz,ezh->evh", left_operand[1], right_operand[0], preferred_element_type=jnp.float32
    )
    return jnp.stack([real_component, imaginary_component])


def to_time(band, inverse):
    flat_band = band.reshape(2 * band.shape[1], band.shape[2], band.shape[3])
    return jnp.einsum("csr,ct->srt", flat_band, inverse, precision=FULL_ACCURACY)


def local(left_traces, right_traces, surf_map, shot_map):
    source_rows, half_size, samples = left_traces.shape
    row_count, receivers = (right_traces.shape[1], right_traces.shape[2])
    bin_count = BINS
    forward, inverse = tables(samples, bin_count)
    left_band = jnp.einsum(
        "ct,skt->csk", forward, left_traces.astype(jnp.float32), precision=FULL_ACCURACY
    ).astype(jnp.bfloat16)
    matches = shot_map[:, None] == jnp.arange(half_size, dtype=jnp.int32)[None, :]
    columns = jnp.sum(jnp.where(matches, surf_map[:, None], 0), axis=0)
    aligned = jnp.take(left_band, columns, axis=2).reshape(2, bin_count, source_rows, half_size)
    right_band = jnp.einsum(
        "ct,qrt->cqr", forward, right_traces[0].astype(jnp.float32), precision=FULL_ACCURACY
    ).astype(jnp.bfloat16)
    right_band = right_band.reshape(2, bin_count, row_count, receivers)
    band = complex_product(aligned, lax.all_gather(right_band, "src", axis=2, tiled=True))
    shared_band = lax.psum_scatter(band, "srf", scatter_dimension=3, tiled=True)
    result = to_time(shared_band, inverse)
    return result.astype(jnp.bfloat16)


def solution(mesh):
    in_specs = (
        P(("grp", "src"), "srf", None),
        P("srf", "src", "grp", None),
        P(("grp", "srf")),
        P(("grp", "srf")),
    )
    out_specs = P(("grp", "src"), "srf", None)
    return jax.shard_map(local, mesh=mesh, in_specs=in_specs, out_specs=out_specs, check_vma=False)
```

profile of v0, /device:TPU:1, one launch (start us, length us, event | category | flops | bytes accessed | tf_op | source)
XLA Modules:
  0.0 294.9 jit_solution(3020097303041725620)
XLA Ops:
  6.5 0.0 copy-start
  6.5 0.0 copy-start.1
  6.5 0.0 copy-start.2
  6.5 0.0 all-gather.2.cloned.1.call-start
  6.6 0.2 fusion.33
  6.8 6.2 %fusion.6 = bf16[80,16,512]{2,0,1:T(8,128)(2,1)S(1)} fusion(bf16[1,16,512,256]{3,2,1,0:T(8,128)(2,1)} %param.5, f32[40,256]{1,0:T(8,128)S(1)} %get-tuple-element.6, f32[40,256]{1,0:T(8,128)S(1)} %get-tuple-element.5), kind=kOutput, calls=%fused_computation.9 | convolution fusion | flops 2013941760 | bytes 5586944 | tf_op jit(solution)/shard_map/ct,qrt->cqr/dot_general | solution.py:54
  13.0 1.8 copy.17
  14.8 0.0 all-gather.2.cloned.1.call-update
  14.8 0.0 reduce-scatter.2.cloned.1.call-start
  14.9 0.0 copy-done
  14.9 1.1 convolution_convert_fusion.1
  16.0 0.3 copy.15
  16.3 0.0 copy-done.1
  16.3 0.0 copy-done.2
  16.3 0.1 select_reduce_fusion
  16.5 0.8 gather_fusion
  17.3 0.5 copy.16
  17.8 237.0 %all-gather.2.cloned.1.call-done = bf16[2,40,256,512]{3,2,1,0:T(8,128)(2,1)} async-done(((bf16[2,40,16,512]{3,2,1,0:T(8,128)(2,1)}), bf16[2,40,256,512]{3,2,1,0:T(8,128)(2,1)}) %all-gather.2.cloned.1.call-update) | async-done | bytes 20971536 | tf_op jit(solution)/shard_map/all_gather | solution.py:58
  254.8 4.9 %fusion = f32[40,8,512]{2,1,0:T(8,128)S(1)} fusion(bf16[2,40,256,512]{3,2,1,0:T(8,128)(2,1)} %all-gather.2.cloned.1.call-done, bf16[256,80,8]{0,2,1:T(8,128)(2,1)S(1)} %copy.16, pred[256]{0:T(512)(128)(4,1)S(1)} %compare_and_fusion), kind=kOutput, calls=%fused_computation.3 | convolution fusion | flops 84049920 | bytes 11469056 | tf_op jit(solution)/shard_map/evz,ezh->evh/dot_general | solution.py:32
  259.7 4.9 %fusion.1 = f32[40,8,512]{2,1,0:T(8,128)S(1)} fusion(bf16[2,40,256,512]{3,2,1,0:T(8,128)(2,1)} %all-gather.2.cloned.1.call-done, bf16[256,80,8]{0,2,1:T(8,128)(2,1)S(1)} %copy.16, pred[256]{0:T(512)(128)(4,1)S(1)} %compare_and_fusion), kind=kOutput, calls=%fused_computation.4 | convolution fusion | flops 84049920 | bytes 11469056 | tf_op jit(solution)/shard_map/evz,ezh->evh/dot_general | solution.py:25
  264.6 5.0 %fusion.12 = f32[1,40,8,512]{3,2,1,0:T(8,128)S(1)} fusion(f32[40,8,512]{2,1,0:T(8,128)S(1)} %fusion, bf16[2,40,256,512]{3,2,1,0:T(8,128)(2,1)} %all-gather.2.cloned.1.call-done, bf16[256,80,8]{0,2,1:T(8,128)(2,1)S(1)} %copy.16, pred[256]{0:T(512)(128)(4,1)S(1)} %compare_and_fusion), kind=kOutput, calls=%fused_computation.15 | convolution fusion | flops 84213760 | bytes 12124416 | tf_op jit(solution)/shard_map/evz,ezh->evh/dot_general | solution.py:30
  269.6 5.0 %fusion.10 = f32[1,40,8,512]{3,2,1,0:T(8,128)S(1)} fusion(f32[40,8,512]{2,1,0:T(8,128)S(1)} %fusion.1, bf16[2,40,256,512]{3,2,1,0:T(8,128)(2,1)} %all-gather.2.cloned.1.call-done, bf16[256,80,8]{0,2,1:T(8,128)(2,1)S(1)} %copy.16, pred[256]{0:T(512)(128)(4,1)S(1)} %compare_and_fusion), kind=kOutput, calls=%fused_computation.13 | convolution fusion | flops 84213760 | bytes 12124416 | tf_op jit(solution)/shard_map/evz,ezh->evh/dot_general | solution.py:27
  274.6 1.2 pad_maximum_fusion
  275.8 0.0 reduce-scatter.2.cloned.1.call-update
  275.8 8.4 %reduce-scatter.2.cloned.1.call-done = f32[2,40,8,256]{3,2,1,0:T(8,128)} async-done(((f32[2,40,8,512]{3,2,1,0:T(8,128)}), f32[2,40,8,256]{3,2,1,0:T(8,128)}) %reduce-scatter.2.cloned.1.call-update) | async-done | bytes 655376 | tf_op jit(solution)/shard_map/reduce_scatter | solution.py:59
  284.2 3.9 %convolution_convert_fusion = bf16[8,256,256]{2,1,0:T(8,128)(2,1)} fusion(f32[80,8,256]{2,1,0:T(8,128)} %bitcast.48, f32[40,256]{1,0:T(8,128)S(1)} %get-tuple-element.6, f32[40,256]{1,0:T(8,128)S(1)} %get-tuple-element.5), kind=kOutput, calls=%fused_computation.10 | convolution fusion | flops 503881728 | bytes 1785856 | tf_op jit(solution)/shard_map/csr,ct->srt/dot_general | solution.py:40
  (4 shorter events, 0.0 us)
Async XLA Ops:
  6.5 8.3 %copy-start = (bf16[8,256,256]{2,1,0:T(8,128)(2,1)S(1)}, bf16[8,256,256]{2,1,0:T(8,128)(2,1)}, u32[]{:S(2)}) copy-start(bf16[8,256,256]{2,1,0:T(8,128)(2,1)} %param.4) | copy-start | bytes 3145732
  6.5 9.8 %copy-start.1 = (s32[256]{0:T(256)S(1)}, s32[256]{0:T(256)}, u32[]{:S(2)}) copy-start(s32[256]{0:T(256)} %param.6) | copy-start | bytes 3076
  6.5 9.8 %copy-start.2 = (s32[256]{0:T(256)S(1)}, s32[256]{0:T(256)}, u32[]{:S(2)}) copy-start(s32[256]{0:T(256)} %param.7) | copy-start | bytes 3076
  6.5 248.3 %all-gather.2.cloned.1.call-start = ((), (), s32[]{:S(2)}) async-start(), calls=%async_computation.1 | async-start | bytes 22282240 | tf_op jit(solution)/shard_map/all_gather | solution.py:58
  14.8 269.4 %reduce-scatter.2.cloned.1.call-start = ((), (), s32[]{:S(2)}) async-start(), calls=%async_computation.2 | async-start | bytes 1966080 | tf_op jit(solution)/shard_map/reduce_scatter | solution.py:59
Sparse Core Ops, SparseCore 0:
  14.9 239.8 all-gather.1
  275.9 8.2 reduce-scatter.1
where the time goes:
time: 295 us
  waiting for transfers between devices  245 us (83%)
  matrix products  30.9 us (10%)
  between operations  13.5 us (5%)
  local copies, waits for them, and re-layouts  3.41 us (1%)
    all_gather x1, waiting for transfers between devices, local(): lax.all_gather(right_band, 'src', axis=2, tiled=True)  237 us
    reduce_scatter x1, waiting for transfers between devices, local(): shared_band = lax.psum_scatter(band, 'srf', scatter_dimension=3, tiled=True)  8.42 us
    dot_general x1, matrix products, local(): jnp.einsum('ct,qrt->cqr', forward, right_traces[0].astype(jnp.float32), p...  6.19 us
  transfers between devices with their start and end apart: 2, of which 2 were waited for; matrix products, arithmetic and copies ran while one was open for 1% of the time, Pallas kernels for 0%

commit v1 on v0

v1 whole, which is shorter than its diff:
```python
import functools
import math

import jax
import jax.numpy as jnp
import ml_dtypes
import numpy as np
from jax import lax
from jax.experimental import pallas as pl
from jax.experimental.pallas import tpu as pltpu
from jax.sharding import PartitionSpec as P

BINS = 40
GROUP = 8
SLOTS = BINS // GROUP
ROW_TILE = 16
F32 = jnp.float32
BF16 = jnp.bfloat16


def split(table):
    high = table.astype(ml_dtypes.bfloat16)
    low = (table - high.astype(np.float64)).astype(ml_dtypes.bfloat16)
    return np.concatenate([high, low], axis=0)


def tables(samples):
    phase = np.arange(1, BINS + 1)[:, None] * np.arange(samples)[None, :] % samples
    angles = phase * (2.0 * math.pi / samples)
    forward = np.stack([np.cos(angles), -np.sin(angles)], axis=1).reshape(2 * BINS, samples)
    return split(forward), split(forward * (2.0 / samples))


def exchange(n, right, left, out, r_in, l_in, part, c_in, z_out, z_in, f_out, f_in,
             r_send, r_recv, l_send, l_recv, c_send, c_recv, z_send, z_recv, f_send, f_recv):
    teams = n // GROUP
    me = lax.axis_index("src")
    core = lax.axis_index("srf")
    other = 1 - core
    team = me // GROUP
    place = me % GROUP
    rows = GROUP * ROW_TILE
    half = part.shape[-1]

    barrier = pltpu.get_barrier_semaphore()

    def greet(d, carry):
        pl.semaphore_signal(barrier, inc=1, device_id={"src": lax.rem(me + d, n)})
        return carry

    lax.fori_loop(1, n, greet, 0)
    pl.semaphore_signal(barrier, inc=1, device_id={"srf": other})
    pl.semaphore_wait(barrier, n)

    def l_copy(d):
        to = lax.rem(me + d, n)
        return pltpu.make_async_remote_copy(
            left.at[to], l_in.at[me], l_send.at[d], l_recv.at[d], device_id={"src": to})

    def r_copy(b, d):
        to = lax.rem(place + d, GROUP)
        return pltpu.make_async_remote_copy(
            right.at[to, b], r_in.at[b, :, place], r_send.at[b, d], r_recv.at[b, d],
            device_id={"src": team * GROUP + to})

    def c_copy(b):
        return pltpu.make_async_remote_copy(
            part.at[b, other], c_in.at[b], c_send.at[b], c_recv.at[b], device_id={"srf": other})

    def z_copy(b, d):
        to = lax.rem(team + d, teams)
        return pltpu.make_async_remote_copy(
            z_out.at[b, to], z_in.at[b, d], z_send.at[b, d], z_recv.at[b, d],
            device_id={"src": to * GROUP + place})

    def f_copy(b, d):
        to = lax.rem(place + d, GROUP)
        return pltpu.make_async_remote_copy(
            f_out.at[b, to], f_in.at[place, b], f_send.at[b, d], f_recv.at[b, d],
            device_id={"src": team * GROUP + to})

    def start_left(d, carry):
        l_copy(d).start()
        return carry

    lax.fori_loop(1, n, start_left, 0)
    for b in range(SLOTS):
        for d in range(1, GROUP):
            r_copy(b, d).start()
    l_in[me] = left[me]
    for b in range(SLOTS):
        r_in[b, :, place] = right[place, b]

    def wait_left(d, carry):
        l_copy(d).wait_recv()
        return carry

    lax.fori_loop(1, n, wait_left, 0)

    def multiply(b):
        for d in range(1, GROUP):
            r_copy(b, d).wait_recv()
        straight = l_in[:, b].reshape(n * ROW_TILE, rows)
        wide = straight.astype(F32).reshape(n, 2, ROW_TILE // 2, rows)
        turned = jnp.concatenate([-wide[:, 1:2], wide[:, 0:1]], axis=1)
        turned = turned.reshape(n * ROW_TILE, rows).astype(BF16)
        real = r_in[b, 0].reshape(rows, 2 * half)
        imag = r_in[b, 1].reshape(rows, 2 * half)
        total = jnp.dot(straight, real, preferred_element_type=F32)
        total += jnp.dot(turned, imag, preferred_element_type=F32)
        part[b, 0] = total[:, :half]
        part[b, 1] = total[:, half:]
        c_copy(b).start()

    def add_cores(b):
        c_copy(b).wait_recv()
        total = part[b, core] + c_in[b]
        part[b, core] = total
        z_out[b] = total.astype(BF16).reshape(teams, rows, half)
        for d in range(1, teams):
            z_copy(b, d).start()

    def add_teams(b):
        total = part[b, core, pl.ds(pl.multiple_of(team * rows, rows), rows), :]
        for d in range(1, teams):
            z_copy(b, d).wait_recv()
            total += z_in[b, d].astype(F32)
        f_out[b] = total.astype(BF16).reshape(GROUP, ROW_TILE, half)
        for d in range(1, GROUP):
            f_copy(b, d).start()
        f_in[place, b] = f_out[b, place]

    for step in range(SLOTS + 2):
        if step < SLOTS:
            multiply(step)
        if 0 <= step - 1 < SLOTS:
            add_cores(step - 1)
        if 0 <= step - 2 < SLOTS:
            add_teams(step - 2)
    for b in range(SLOTS):
        for d in range(1, GROUP):
            f_copy(b, d).wait_recv()
    out[...] = f_in[...]

    def end_left(d, carry):
        l_copy(d).wait_send()
        return carry

    lax.fori_loop(1, n, end_left, 0)
    for b in range(SLOTS):
        c_copy(b).wait_send()
        for d in range(1, GROUP):
            r_copy(b, d).wait_send()
            f_copy(b, d).wait_send()
        for d in range(1, teams):
            z_copy(b, d).wait_send()


def band_of(n, right, left):
    teams = n // GROUP
    rows = GROUP * ROW_TILE
    receivers = right.shape[-1]
    half = receivers // 2
    dma = pltpu.SemaphoreType.DMA
    vmem = pl.BlockSpec(memory_space=pltpu.VMEM)
    return pl.pallas_call(
        functools.partial(exchange, n),
        out_shape=jax.ShapeDtypeStruct((GROUP, SLOTS, ROW_TILE, half), BF16),
        in_specs=[vmem, vmem],
        out_specs=vmem,
        scratch_shapes=[
            pltpu.VMEM((SLOTS, 2, GROUP, ROW_TILE, receivers), BF16),
            pltpu.VMEM((n, SLOTS, ROW_TILE, rows), BF16),
            pltpu.VMEM((SLOTS, 2, n * ROW_TILE, half), F32),
            pltpu.VMEM((SLOTS, n * ROW_TILE, half), F32),
            pltpu.VMEM((SLOTS, teams, rows, half), BF16),
            pltpu.VMEM((SLOTS, teams, rows, half), BF16),
            pltpu.VMEM((SLOTS, GROUP, ROW_TILE, half), BF16),
            pltpu.VMEM((GROUP, SLOTS, ROW_TILE, half), BF16),
            dma((SLOTS, GROUP)), dma((SLOTS, GROUP)),
            dma((n,)), dma((n,)),
            dma((SLOTS,)), dma((SLOTS,)),
            dma((SLOTS, teams)), dma((SLOTS, teams)),
            dma((SLOTS, GROUP)), dma((SLOTS, GROUP)),
        ],
        compiler_params=pltpu.CompilerParams(
            collective_id=0, has_side_effects=True, vmem_limit_bytes=48 * 2**20),
        cost_estimate=pl.CostEstimate(
            flops=2 * SLOTS * n * ROW_TILE * 2 * rows * receivers,
            bytes_accessed=2 * right.size * 2, transcendentals=0),
    )(right, left)


def local(n, left_traces, right_traces, surf_map, shot_map):
    sources, half_size, samples = left_traces.shape
    row_count, receivers = right_traces.shape[1:3]
    teams = n // GROUP
    values = 2 * BINS
    forward, inverse = tables(samples)

    def spectra(traces):
        both = [
            jnp.einsum("ct,abt->cab", forward[part], traces, preferred_element_type=F32)
            for part in (slice(None, values), slice(values, None))
        ]
        return (both[0] + both[1]).astype(BF16)

    pad = ROW_TILE - row_count
    right = spectra(right_traces[0])
    if pad:
        right = jnp.pad(right, ((0, 0), (0, pad), (0, 0)))
    right = right.reshape(GROUP, SLOTS, 2, ROW_TILE, receivers)

    columns = jnp.arange(half_size, dtype=jnp.int32)
    surf_hot = (surf_map[:, None] == columns[None, :]).astype(BF16)
    shot_hot = (shot_map[:, None] == columns[None, :]).astype(BF16)
    move = jnp.einsum("jk,jq->kq", surf_hot, shot_hot, preferred_element_type=F32).astype(BF16)
    left = spectra(left_traces)
    left = jnp.einsum("csk,kq->csq", left, move, preferred_element_type=F32).astype(BF16)
    left = left.reshape(GROUP, SLOTS, 2, sources, teams, GROUP, row_count)
    if pad:
        left = jnp.pad(left, ((0, 0),) * 6 + ((0, pad),))
    left = left.transpose(4, 0, 1, 2, 3, 5, 6).reshape(n, SLOTS, ROW_TILE, GROUP * ROW_TILE)

    band = band_of(n, right, left).reshape(BINS * 2, sources, receivers // 2)
    result = [
        jnp.einsum("csr,ct->srt", band, inverse[part], preferred_element_type=F32)
        for part in (slice(None, values), slice(values, None))
    ]
    return (result[0] + result[1]).astype(BF16)


def solution(mesh):
    in_specs = (
        P(("grp", "src"), "srf", None),
        P("srf", "src", "grp", None),
        P(("grp", "srf")),
        P(("grp", "srf")),
    )
    out_specs = P(("grp", "src"), "srf", None)
    body = functools.partial(local, mesh.shape["src"])
    return jax.shard_map(body, mesh=mesh, in_specs=in_specs, out_specs=out_specs, check_vma=False)
```

time: 295 us -> 69.6 us (0.24)
  the two profiles are of different devices: /device:TPU:1 before, /device:TPU:0 now
where the time goes in v1:
time: 69.6 us; the launch traced here: 69.2 us
  Pallas kernels  46.2 us (66%)
  local copies, waits for them, and re-layouts  12.3 us (18%)
  matrix products  10.6 us (15%)
    pallas_call x1, Pallas kernels, band_of(): pl.pallas_call(functools.partial(exchange, n), out_shape=jax.ShapeDtypeSt...  46.2 us
    dot_general x4, matrix products, spectra(): jnp.einsum('ct,abt->cab', forward[part], traces, preferred_element_type=F32)  7.56 us
    reshape x2, local copies, waits for them, and re-layouts, local(): left = left.reshape(GROUP, SLOTS, 2, sources, teams, GROUP, row_count)  6.84 us
    reshape x1, local copies, waits for them, and re-layouts, local(): left.transpose(4, 0, 1, 2, 3, 5, 6)  3.51 us
    dot_general x2, matrix products, local(): jnp.einsum('csr,ct->srt', band, inverse[part], preferred_element_type=F32)  1.92 us

profile of v1, /device:TPU:0, one launch (start us, length us, event | category | flops | bytes accessed | tf_op | source)
XLA Modules:
  0.0 69.2 jit_solution(5781999795234740035)
XLA Ops:
  0.0 0.0 copy-start
  0.0 0.0 copy-start.6
  0.0 1.2 %copy-done = bf16[8,256,256]{2,1,0:T(8,128)(2,1)S(1)} copy-done((bf16[8,256,256]{2,1,0:T(8,128)(2,1)S(1)}, bf16[8,256,256]{2,1,0:T(8,128)(2,1)}, u32[]{:S(2)}) %copy-start) | copy-done | bytes 1048600
  1.2 0.0 copy-start.7
  1.2 1.2 %fusion.17 = f32[80,8,256]{2,0,1:T(8,128)S(1)} fusion(bf16[80,256,1]{1,0,2:T(8,128)(2,1)} %constant.15, bf16[8,256,256]{2,1,0:T(8,128)(2,1)S(1)} %copy-done), kind=kOutput, calls=%fused_computation.20 | convolution fusion | flops 83886080 | bytes 1744896 | tf_op jit(solution)/shard_map/ct,abt->cab/dot_general | solution.py:203
  2.5 1.2 %fusion.16 = f32[80,8,256]{2,0,1:T(8,128)S(1)} fusion(bf16[80,256,1]{1,0,2:T(8,128)(2,1)} %constant.14, bf16[8,256,256]{2,1,0:T(8,128)(2,1)S(1)} %copy-done), kind=kOutput, calls=%fused_computation.19 | convolution fusion | flops 83886080 | bytes 1744896 | tf_op jit(solution)/shard_map/ct,abt->cab/dot_general | solution.py:203
  3.7 0.0 copy-done.6
  3.7 0.0 copy-done.7
  3.7 1.1 %convolution_convert_fusion = bf16[80,8,256]{2,1,0:T(8,128)(2,1)S(1)} fusion(f32[80,8,256]{2,0,1:T(8,128)S(1)} %fusion.17, f32[80,8,256]{2,0,1:T(8,128)S(1)} %fusion.16, s32[256]{0:T(256)S(1)} %copy-done.6, s32[256]{0:T(256)S(1)} %copy-done.7), kind=kOutput, calls=%fused_computation.7 | convolution fusion | flops 118128640 | bytes 1640448 | tf_op jit(solution)/shard_map/csk,kq->csq/dot_general | solution.py:219
  4.8 2.8 %reshape.15 = bf16[8,5,2,8,2,8,16]{6,5,4,3,2,1,0:T(8,128)(2,1)} reshape(bf16[80,8,256]{2,1,0:T(8,128)(2,1)S(1)} %convolution_convert_fusion) | data formatting | bytes 655360 | tf_op jit(solution)/shard_map/reshape | solution.py:220
  7.6 4.0 %copy.28 = bf16[8,5,2,8,2,8,16]{6,5,3,2,1,0,4:T(8,128)(2,1)} copy(bf16[8,5,2,8,2,8,16]{6,5,4,3,2,1,0:T(8,128)(2,1)} %reshape.15) | data formatting | bytes 655360 | tf_op jit(solution)/shard_map/reshape | solution.py:220
  11.6 0.0 copy-start.2
  11.6 3.5 %reshape.16.left = bf16[16,5,16,128]{3,2,1,0:T(8,128)(2,1)S(1)} reshape(bf16[2,8,5,2,8,8,16]{6,5,4,3,2,1,0:T(8,128)(2,1)} %bitcast.33) | data formatting | bytes 655360 | tf_op jit(solution)/shard_map/reshape | solution.py:223
  15.1 0.0 copy-done.2
  15.2 0.0 copy-start.1
  15.2 0.0 copy-start.3
  15.2 3.7 %fusion = f32[80,16,512]{2,0,1:T(8,128)S(1)} fusion(bf16[80,256,1]{1,0,2:T(8,128)(2,1)S(1)} %copy-done.2, bf16[1,16,512,256]{3,2,1,0:T(8,128)(2,1)} %param.11), kind=kOutput, calls=%fused_computation | convolution fusion | flops 335544320 | bytes 6856704 | tf_op jit(solution)/shard_map/ct,abt->cab/dot_general | solution.py:203
  18.9 0.0 copy-done.1
  18.9 0.0 copy-done.3
  18.9 1.4 %add_convert_fusion = bf16[80,16,512]{2,0,1:T(8,128)(2,1)S(1)} fusion(f32[80,16,512]{2,0,1:T(8,128)S(1)} %fusion, bf16[80,256,1]{1,0,2:T(8,128)(2,1)S(1)} %copy-done.3, bf16[1,16,512,256]{3,2,1,0:T(8,128)(2,1)S(1)} %copy-done.1), kind=kOutput, calls=%fused_computation.5 | convolution fusion | flops 336855040 | bytes 8167424 | tf_op jit(solution)/shard_map/ct,abt->cab/dot_general | solution.py:203
  20.3 0.0 copy-start.5
  20.3 0.7 %copy.11 = bf16[80,16,512]{2,1,0:T(8,128)(2,1)S(1)} copy(bf16[80,16,512]{2,0,1:T(8,128)(2,1)S(1)} %add_convert_fusion) | data formatting | bytes 2621440 | tf_op jit(solution)/shard_map/convert_element_type | solution.py:206
  21.1 0.0 copy-start.4
  21.1 46.2 %shard_map.100 = bf16[8,5,16,256]{3,2,1,0:T(8,128)(2,1)S(1)} custom-call(bf16[8,5,2,16,512]{4,3,2,1,0:T(8,128)(2,1)S(1)} %bitcast.30, bf16[16,5,16,128]{3,2,1,0:T(8,128)(2,1)S(1)} %reshape.16.left), custom_call_target="tpu_custom_call" | custom-call | flops 335544320 | bytes 2621440 | tf_op jit(solution)/shard_map/pallas_call | solution.py:166
  67.3 0.0 copy-done.5
  67.3 0.5 fusion.10
  67.7 0.0 copy-done.4
  67.8 1.4 %add_convert_fusion.1 = bf16[8,256,256]{2,1,0:T(8,128)(2,1)} fusion(f32[8,256,256]{2,1,0:T(8,128)S(1)} %fusion.10, bf16[80,256,1]{1,0,2:T(8,128)(2,1)S(1)} %copy-done.4, bf16[80,8,256]{2,1,0:T(8,128)(2,1)S(1)} %bitcast.32), kind=kOutput, calls=%fused_computation.6 | convolution fusion | flops 84934656 | bytes 3514368 | tf_op jit(solution)/shard_map/csr,ct->srt/dot_general | solution.py:227
Async XLA Ops:
  0.0 1.2 %copy-start = (bf16[8,256,256]{2,1,0:T(8,128)(2,1)S(1)}, bf16[8,256,256]{2,1,0:T(8,128)(2,1)}, u32[]{:S(2)}) copy-start(bf16[8,256,256]{2,1,0:T(8,128)(2,1)} %param.10) | copy-start | bytes 3145732
  0.0 3.7 %copy-start.6 = (s32[256]{0:T(256)S(1)}, s32[256]{0:T(256)}, u32[]{:S(2)}) copy-start(s32[256]{0:T(256)} %param.13) | copy-start | bytes 3076
  1.2 2.5 %copy-start.7 = (s32[256]{0:T(256)S(1)}, s32[256]{0:T(256)}, u32[]{:S(2)}) copy-start(s32[256]{0:T(256)} %param.12) | copy-start | bytes 3076
  11.6 3.5 %copy-start.2 = (bf16[80,256,1]{1,0,2:T(8,128)(2,1)S(1)}, bf16[80,256,1]{1,0,2:T(8,128)(2,1)}, u32[]{:S(2)}) copy-start(bf16[80,256,1]{1,0,2:T(8,128)(2,1)} %constant.15) | copy-start | bytes 122884
  15.2 3.7 %copy-start.1 = (bf16[1,16,512,256]{3,2,1,0:T(8,128)(2,1)S(1)}, bf16[1,16,512,256]{3,2,1,0:T(8,128)(2,1)}, u32[]{:S(2)}) copy-start(bf16[1,16,512,256]{3,2,1,0:T(8,128)(2,1)} %param.11) | copy-start | bytes 12582916
  15.2 3.7 %copy-start.3 = (bf16[80,256,1]{1,0,2:T(8,128)(2,1)S(1)}, bf16[80,256,1]{1,0,2:T(8,128)(2,1)}, u32[]{:S(2)}) copy-start(bf16[80,256,1]{1,0,2:T(8,128)(2,1)} %constant.14) | copy-start | bytes 122884
  20.3 46.9 %copy-start.5 = (bf16[80,256,1]{1,0,2:T(8,128)(2,1)S(1)}, bf16[80,256,1]{1,0,2:T(8,128)(2,1)}, u32[]{:S(2)}) copy-start(bf16[80,256,1]{1,0,2:T(8,128)(2,1)} %constant.16) | copy-start | bytes 122884
  21.1 46.7 %copy-start.4 = (bf16[80,256,1]{1,0,2:T(8,128)(2,1)S(1)}, bf16[80,256,1]{1,0,2:T(8,128)(2,1)}, u32[]{:S(2)}) copy-start(bf16[80,256,1]{1,0,2:T(8,128)(2,1)} %constant.17) | copy-start | bytes 122884

commit v2 on v1

--- a/solution.py
+++ b/solution.py
@@ -14,6 +14,7 @@
 GROUP = 8
 SLOTS = BINS // GROUP
 ROW_TILE = 16
+LANES = 128
 F32 = jnp.float32
 BF16 = jnp.bfloat16
 
@@ -31,7 +32,11 @@
     return split(forward), split(forward * (2.0 / samples))
 
 
-def exchange(n, right, left, out, r_in, l_in, part, c_in, z_out, z_in, f_out, f_in,
+NT = (((1,), (1,)), ((), ()))
+
+
+def exchange(n, left_ref, right_ref, surf_ref, shot_ref, table_ref, out, traces, lines, right, left,
+             r_in, l_in, part, c_in, z_out, z_in, f_out, f_in, fetch_sem,
              r_send, r_recv, l_send, l_recv, c_send, c_recv, z_send, z_recv, f_send, f_recv):
     teams = n // GROUP
     me = lax.axis_index("src")
@@ -41,6 +46,9 @@
     place = me % GROUP
     rows = GROUP * ROW_TILE
     half = part.shape[-1]
+    values = 2 * BINS
+    sources, half_size, _ = left_ref.shape
+    row_count, receivers = right_ref.shape[1:3]
 
     barrier = pltpu.get_barrier_semaphore()
 
@@ -50,6 +58,28 @@
 
     lax.fori_loop(1, n, greet, 0)
     pl.semaphore_signal(barrier, inc=1, device_id={"srf": other})
+    fetch = pltpu.make_async_copy(right_ref.at[0], traces, fetch_sem)
+    fetch.start()
+
+    def spectrum(block):
+        both = lax.dot_general(table_ref[...], block, NT, preferred_element_type=F32)
+        return (both[:values] + both[values:]).astype(BF16)
+
+    at = lax.broadcasted_iota(jnp.int32, (half_size, half_size), 0)
+    surf_hot = (at == surf_ref[...]).astype(F32).astype(BF16)
+    spot = lax.broadcasted_iota(jnp.int32, (teams * rows, half_size), 0)
+    shot = shot_ref[...]
+    shot_spot = shot // row_count * ROW_TILE + shot % row_count
+    shot_hot = (spot == shot_spot).astype(F32).astype(BF16)
+    move = lax.dot_general(surf_hot, shot_hot, NT, preferred_element_type=F32).astype(BF16)
+    for s in range(sources):
+        moved = jnp.dot(spectrum(left_ref[s]), move, preferred_element_type=F32)
+        for t in range(teams):
+            lines[t, pl.ds(s, values, stride=sources), :] = moved[:, t * rows:(t + 1) * rows]
+    for t in range(teams):
+        block = lines[t, :values * sources].astype(BF16)
+        left[t * GROUP:(t + 1) * GROUP] = block.reshape(GROUP, SLOTS, ROW_TILE, rows)
+
     pl.semaphore_wait(barrier, n)
 
     def l_copy(d):
@@ -84,6 +114,17 @@
         return carry
 
     lax.fori_loop(1, n, start_left, 0)
+
+    fetch.wait()
+    if row_count < ROW_TILE:
+        lines[...] = jnp.zeros_like(lines)
+    for q in range(row_count):
+        bands = spectrum(traces[q]).astype(F32)
+        for t in range(receivers // LANES):
+            lines[t, pl.ds(q, values, stride=ROW_TILE), :] = bands[:, t * LANES:(t + 1) * LANES]
+    for t in range(receivers // LANES):
+        block = lines[t].astype(BF16).reshape(GROUP, SLOTS, 2, ROW_TILE, LANES)
+        right[..., t * LANES:(t + 1) * LANES] = block
     for b in range(SLOTS):
         for d in range(1, GROUP):
             r_copy(b, d).start()
@@ -156,19 +197,23 @@
             z_copy(b, d).wait_send()
 
 
-def band_of(n, right, left):
+def band_of(n, left, right, surf_map, shot_map, table):
     teams = n // GROUP
     rows = GROUP * ROW_TILE
-    receivers = right.shape[-1]
+    receivers = right.shape[2]
     half = receivers // 2
     dma = pltpu.SemaphoreType.DMA
     vmem = pl.BlockSpec(memory_space=pltpu.VMEM)
     return pl.pallas_call(
         functools.partial(exchange, n),
         out_shape=jax.ShapeDtypeStruct((GROUP, SLOTS, ROW_TILE, half), BF16),
-        in_specs=[vmem, vmem],
+        in_specs=[vmem, pl.BlockSpec(memory_space=pl.ANY), vmem, vmem, vmem],
         out_specs=vmem,
         scratch_shapes=[
+            pltpu.VMEM(right.shape[1:], BF16),
+            pltpu.VMEM((max(teams, receivers // LANES), 2 * BINS * ROW_TILE, LANES), F32),
+            pltpu.VMEM((GROUP, SLOTS, 2, ROW_TILE, receivers), BF16),
+            pltpu.VMEM((n, SLOTS, ROW_TILE, rows), BF16),
             pltpu.VMEM((SLOTS, 2, GROUP, ROW_TILE, receivers), BF16),
             pltpu.VMEM((n, SLOTS, ROW_TILE, rows), BF16),
             pltpu.VMEM((SLOTS, 2, n * ROW_TILE, half), F32),
@@ -177,6 +222,7 @@
             pltpu.VMEM((SLOTS, teams, rows, half), BF16),
             pltpu.VMEM((SLOTS, GROUP, ROW_TILE, half), BF16),
             pltpu.VMEM((GROUP, SLOTS, ROW_TILE, half), BF16),
+            dma(()),
             dma((SLOTS, GROUP)), dma((SLOTS, GROUP)),
             dma((n,)), dma((n,)),
             dma((SLOTS,)), dma((SLOTS,)),
@@ -188,41 +234,16 @@
         cost_estimate=pl.CostEstimate(
             flops=2 * SLOTS * n * ROW_TILE * 2 * rows * receivers,
             bytes_accessed=2 * right.size * 2, transcendentals=0),
-    )(right, left)
+    )(left, right, surf_map, shot_map, table)
 
 
 def local(n, left_traces, right_traces, surf_map, shot_map):
-    sources, half_size, samples = left_traces.shape
-    row_count, receivers = right_traces.shape[1:3]
-    teams = n // GROUP
+    sources, _, samples = left_traces.shape
+    receivers = right_traces.shape[2]
     values = 2 * BINS
     forward, inverse = tables(samples)
-
-    def spectra(traces):
-        both = [
-            jnp.einsum("ct,abt->cab", forward[part], traces, preferred_element_type=F32)
-            for part in (slice(None, values), slice(values, None))
-        ]
-        return (both[0] + both[1]).astype(BF16)
-
-    pad = ROW_TILE - row_count
-    right = spectra(right_traces[0])
-    if pad:
-        right = jnp.pad(right, ((0, 0), (0, pad), (0, 0)))
-    right = right.reshape(GROUP, SLOTS, 2, ROW_TILE, receivers)
-
-    columns = jnp.arange(half_size, dtype=jnp.int32)
-    surf_hot = (surf_map[:, None] == columns[None, :]).astype(BF16)
-    shot_hot = (shot_map[:, None] == columns[None, :]).astype(BF16)
-    move = jnp.einsum("jk,jq->kq", surf_hot, shot_hot, preferred_element_type=F32).astype(BF16)
-    left = spectra(left_traces)
-    left = jnp.einsum("csk,kq->csq", left, move, preferred_element_type=F32).astype(BF16)
-    left = left.reshape(GROUP, SLOTS, 2, sources, teams, GROUP, row_count)
-    if pad:
-        left = jnp.pad(left, ((0, 0),) * 6 + ((0, pad),))
-    left = left.transpose(4, 0, 1, 2, 3, 5, 6).reshape(n, SLOTS, ROW_TILE, GROUP * ROW_TILE)
-
-    band = band_of(n, right, left).reshape(BINS * 2, sources, receivers // 2)
+    band = band_of(n, left_traces, right_traces, surf_map[None], shot_map[None], jnp.asarray(forward))
+    band = band.reshape(values, sources, receivers // 2)
     result = [
         jnp.einsum("csr,ct->srt", band, inverse[part], preferred_element_type=F32)
         for part in (slice(None, values), slice(values, None))

time: 69.6 us -> 54.5 us (0.78)
  matrix products: 10.6 us -> 1.91 us
  local copies, waits for them, and re-layouts: 12.3 us -> 5.95 us
    reshape x3 -> x0, local copies, waits for them, and re-layouts: 10.3 us -> none  [the longest x2 6.84 us: local(): left = left.reshape(GROUP, SLOTS, 2, sources, teams, GROUP, row_count)]
    dot_general x5 -> x0, matrix products: 8.65 us -> none  [the longest x4 7.56 us: spectra(): jnp.einsum('ct,abt->cab', forward[part], traces, preferred_element_type=F32)]
    unnamed x16 -> x14, local copies, waits for them, and re-layouts: 1.26 us -> 5.95 us
    convert_element_type x1 -> x0, local copies, waits for them, and re-layouts: 0.72 us -> none  [spectra(): return (both[0] + both[1]).astype(BF16)]
where the time goes in v2:
time: 54.5 us; the launch traced here: 54.2 us
  Pallas kernels  46.3 us (85%)
  local copies, waits for them, and re-layouts  5.95 us (11%)
  matrix products  1.91 us (4%)
    pallas_call x1, Pallas kernels, band_of(): pl.pallas_call(functools.partial(exchange, n), out_shape=jax.ShapeDtypeSt...  46.3 us
    unnamed x14, local copies, waits for them, and re-layouts  5.95 us
    dot_general x2, matrix products, local(): jnp.einsum('csr,ct->srt', band, inverse[part], preferred_element_type=F32)  1.91 us

profile of v2, /device:TPU:0, one launch (start us, length us, event | category | flops | bytes accessed | tf_op | source)
XLA Modules:
  0.0 54.2 jit_solution(11438228471384862369)
XLA Ops:
  0.0 0.0 copy-start
  0.0 2.2 %copy-done = bf16[1,16,512,256]{3,2,1,0:T(8,128)(2,1)S(1)} copy-done((bf16[1,16,512,256]{3,2,1,0:T(8,128)(2,1)S(1)}, bf16[1,16,512,256]{3,2,1,0:T(8,128)(2,1)}, u32[]{:S(2)}) %copy-start) | copy-done | bytes 4194328
  2.2 0.0 copy-start.1
  2.2 1.2 %copy-done.1 = bf16[8,256,256]{2,1,0:T(8,128)(2,1)S(1)} copy-done((bf16[8,256,256]{2,1,0:T(8,128)(2,1)S(1)}, bf16[8,256,256]{2,1,0:T(8,128)(2,1)}, u32[]{:S(2)}) %copy-start.1) | copy-done | bytes 1048600
  3.4 0.0 copy-start.2
  3.4 0.9 %copy-done.2 = bf16[160,256]{1,0:T(8,128)(2,1)S(1)} copy-done((bf16[160,256]{1,0:T(8,128)(2,1)S(1)}, bf16[160,256]{1,0:T(8,128)(2,1)}, u32[]{:S(2)}) %copy-start.2) | copy-done | bytes 81944
  4.3 0.0 copy-start.3
  4.3 0.7 %copy-done.3 = s32[256]{0:T(256)S(1)} copy-done((s32[256]{0:T(256)S(1)}, s32[256]{0:T(256)}, u32[]{:S(2)}) %copy-start.3) | copy-done | bytes 1048
  5.0 0.0 copy-start.4
  5.0 0.7 %copy-done.4 = s32[256]{0:T(256)S(1)} copy-done((s32[256]{0:T(256)S(1)}, s32[256]{0:T(256)}, u32[]{:S(2)}) %copy-start.4) | copy-done | bytes 1048
  5.7 0.0 copy-start.6
  5.7 46.3 %shard_map.73 = bf16[8,5,16,256]{3,2,1,0:T(8,128)(2,1)S(1)} custom-call(bf16[8,256,256]{2,1,0:T(8,128)(2,1)S(1)} %copy-done.1, bf16[1,16,512,256]{3,2,1,0:T(8,128)(2,1)S(1)} %copy-done, s32[1,256]{1,0:T(1,128)S(1)} %bitcast.9, s32[1,256]{1,0:T(1,128)S(1)} %bitcast.10, bf16[160,256]{1,0:T(8,128)(2,1)S(1)} %copy-done.2), custom_call_target="tpu_custom_call" | custom-call | flops 335544320 | bytes 8388608 | tf_op jit(solution)/shard_map/pallas_call | solution.py:207
  52.0 0.0 copy-start.5
  52.0 0.0 copy-done.6
  52.0 0.5 fusion.1
  52.5 0.3 copy-done.5
  52.7 1.4 %add_convert_fusion = bf16[8,256,256]{2,1,0:T(8,128)(2,1)} fusion(f32[8,256,256]{2,1,0:T(8,128)S(1)} %fusion.1, bf16[80,256,1]{1,0,2:T(8,128)(2,1)S(1)} %copy-done.5, bf16[80,8,256]{2,1,0:T(8,128)(2,1)S(1)} %bitcast.8), kind=kOutput, calls=%fused_computation | convolution fusion | flops 84934656 | bytes 3514368 | tf_op jit(solution)/shard_map/csr,ct->srt/dot_general | solution.py:248
Async XLA Ops:
  0.0 2.2 %copy-start = (bf16[1,16,512,256]{3,2,1,0:T(8,128)(2,1)S(1)}, bf16[1,16,512,256]{3,2,1,0:T(8,128)(2,1)}, u32[]{:S(2)}) copy-start(bf16[1,16,512,256]{3,2,1,0:T(8,128)(2,1)} %right_ref.1) | copy-start | bytes 12582916
  2.2 1.2 %copy-start.1 = (bf16[8,256,256]{2,1,0:T(8,128)(2,1)S(1)}, bf16[8,256,256]{2,1,0:T(8,128)(2,1)}, u32[]{:S(2)}) copy-start(bf16[8,256,256]{2,1,0:T(8,128)(2,1)} %left_ref.1) | copy-start | bytes 3145732
  3.4 0.9 %copy-start.2 = (bf16[160,256]{1,0:T(8,128)(2,1)S(1)}, bf16[160,256]{1,0:T(8,128)(2,1)}, u32[]{:S(2)}) copy-start(bf16[160,256]{1,0:T(8,128)(2,1)} %constant.6.clone.table_ref) | copy-start | bytes 245764
  4.3 0.7 %copy-start.3 = (s32[256]{0:T(256)S(1)}, s32[256]{0:T(256)}, u32[]{:S(2)}) copy-start(s32[256]{0:T(256)} %param.9) | copy-start | bytes 3076
  5.0 0.7 %copy-start.4 = (s32[256]{0:T(256)S(1)}, s32[256]{0:T(256)}, u32[]{:S(2)}) copy-start(s32[256]{0:T(256)} %param.10) | copy-start | bytes 3076
  5.7 46.3 %copy-start.6 = (bf16[80,256,1]{1,0,2:T(8,128)(2,1)S(1)}, bf16[80,256,1]{1,0,2:T(8,128)(2,1)}, u32[]{:S(2)}) copy-start(bf16[80,256,1]{1,0,2:T(8,128)(2,1)} %constant.11) | copy-start | bytes 122884
  52.0 0.8 %copy-start.5 = (bf16[80,256,1]{1,0,2:T(8,128)(2,1)S(1)}, bf16[80,256,1]{1,0,2:T(8,128)(2,1)}, u32[]{:S(2)}) copy-start(bf16[80,256,1]{1,0,2:T(8,128)(2,1)} %constant.12) | copy-start | bytes 122884

commit v3 on v2

--- a/solution.py
+++ b/solution.py
@@ -15,6 +15,10 @@
 SLOTS = BINS // GROUP
 ROW_TILE = 16
 LANES = 128
+FIRST = 3
+EARLY = 6
+AHEAD = 4
+GAP = 3
 F32 = jnp.float32
 BF16 = jnp.bfloat16
 
@@ -35,8 +39,9 @@
 NT = (((1,), (1,)), ((), ()))
 
 
-def exchange(n, left_ref, right_ref, surf_ref, shot_ref, table_ref, out, traces, lines, right, left,
-             r_in, l_in, part, c_in, z_out, z_in, f_out, f_in, fetch_sem,
+def exchange(n, left_hbm, right_hbm, surf_hbm, shot_hbm, table_hbm, out, left_ref, traces, surf_ref,
+             shot_ref, table_ref, lines, right, left,
+             r_in, l_in, l_turn, part, c_in, z_out, z_in, f_out, f_in, fetch_sem,
              r_send, r_recv, l_send, l_recv, c_send, c_recv, z_send, z_recv, f_send, f_recv):
     teams = n // GROUP
     me = lax.axis_index("src")
@@ -48,7 +53,13 @@
     half = part.shape[-1]
     values = 2 * BINS
     sources, half_size, _ = left_ref.shape
-    row_count, receivers = right_ref.shape[1:3]
+    row_count, receivers = right_hbm.shape[1:3]
+
+    pairs = [(surf_hbm, surf_ref), (shot_hbm, shot_ref), (table_hbm, table_ref), (left_hbm, left_ref),
+             (right_hbm.at[0], traces)]
+    fetches = [pltpu.make_async_copy(a, b, fetch_sem.at[i]) for i, (a, b) in enumerate(pairs)]
+    for fetch in fetches:
+        fetch.start()
 
     barrier = pltpu.get_barrier_semaphore()
 
@@ -58,13 +69,12 @@
 
     lax.fori_loop(1, n, greet, 0)
     pl.semaphore_signal(barrier, inc=1, device_id={"srf": other})
-    fetch = pltpu.make_async_copy(right_ref.at[0], traces, fetch_sem)
-    fetch.start()
-
     def spectrum(block):
         both = lax.dot_general(table_ref[...], block, NT, preferred_element_type=F32)
         return (both[:values] + both[values:]).astype(BF16)
 
+    for fetch in fetches[:4]:
+        fetch.wait()
     at = lax.broadcasted_iota(jnp.int32, (half_size, half_size), 0)
     surf_hot = (at == surf_ref[...]).astype(F32).astype(BF16)
     spot = lax.broadcasted_iota(jnp.int32, (teams * rows, half_size), 0)
@@ -87,11 +97,18 @@
         return pltpu.make_async_remote_copy(
             left.at[to], l_in.at[me], l_send.at[d], l_recv.at[d], device_id={"src": to})
 
-    def r_copy(b, d):
+    units = [(part_index, b) for part_index in range(2) for b in range(SLOTS)]
+
+    def r_copy(u, d):
         to = lax.rem(place + d, GROUP)
-        return pltpu.make_async_remote_copy(
-            right.at[to, b], r_in.at[b, :, place], r_send.at[b, d], r_recv.at[b, d],
+        side, b = units[u]
+        return pltpu.make_async_remote_copy(
+            right.at[side, to, b], r_in.at[side, b, :, place], r_send.at[u, d], r_recv.at[u, d],
             device_id={"src": team * GROUP + to})
+
+    def start_right(u):
+        for d in range(1, GROUP):
+            r_copy(u, d).start()
 
     def c_copy(b):
         return pltpu.make_async_remote_copy(
@@ -115,43 +132,50 @@
 
     lax.fori_loop(1, n, start_left, 0)
 
-    fetch.wait()
+    fetches[4].wait()
     if row_count < ROW_TILE:
         lines[...] = jnp.zeros_like(lines)
-    for q in range(row_count):
-        bands = spectrum(traces[q]).astype(F32)
-        for t in range(receivers // LANES):
-            lines[t, pl.ds(q, values, stride=ROW_TILE), :] = bands[:, t * LANES:(t + 1) * LANES]
-    for t in range(receivers // LANES):
-        block = lines[t].astype(BF16).reshape(GROUP, SLOTS, 2, ROW_TILE, LANES)
-        right[..., t * LANES:(t + 1) * LANES] = block
-    for b in range(SLOTS):
-        for d in range(1, GROUP):
-            r_copy(b, d).start()
+    for side in range(2):
+        for q in range(row_count):
+            bands = spectrum(traces[q, side * half:(side + 1) * half]).astype(F32)
+            for t in range(half // LANES):
+                lines[side * (half // LANES) + t, pl.ds(q, values, stride=ROW_TILE), :] = (
+                    bands[:, t * LANES:(t + 1) * LANES])
+        for t in range(half // LANES):
+            block = lines[side * (half // LANES) + t].astype(BF16)
+            right[side, ..., t * LANES:(t + 1) * LANES] = block.reshape(
+                GROUP, SLOTS, 2, ROW_TILE, LANES)
+        for u in range(FIRST) if side == 0 else range(FIRST, EARLY):
+            start_right(u)
+        for b in range(SLOTS):
+            r_in[side, b, :, place] = right[side, place, b]
     l_in[me] = left[me]
-    for b in range(SLOTS):
-        r_in[b, :, place] = right[place, b]
 
     def wait_left(d, carry):
         l_copy(d).wait_recv()
         return carry
 
     lax.fori_loop(1, n, wait_left, 0)
-
-    def multiply(b):
-        for d in range(1, GROUP):
-            r_copy(b, d).wait_recv()
+    for b in range(SLOTS):
+        wide = l_in[:, b].astype(F32).reshape(n, 2, ROW_TILE // 2, rows)
+        turned = jnp.concatenate([-wide[:, 1:2], wide[:, 0:1]], axis=1)
+        l_turn[b] = turned.reshape(n * ROW_TILE, rows).astype(BF16)
+
+    def multiply(u):
+        side, b = units[u]
+        for d in range(1, GROUP):
+            r_copy(u, d).wait_recv()
+        if EARLY <= u + AHEAD < len(units):
+            start_right(u + AHEAD)
         straight = l_in[:, b].reshape(n * ROW_TILE, rows)
-        wide = straight.astype(F32).reshape(n, 2, ROW_TILE // 2, rows)
-        turned = jnp.concatenate([-wide[:, 1:2], wide[:, 0:1]], axis=1)
-        turned = turned.reshape(n * ROW_TILE, rows).astype(BF16)
-        real = r_in[b, 0].reshape(rows, 2 * half)
-        imag = r_in[b, 1].reshape(rows, 2 * half)
+        real = r_in[side, b, 0].reshape(rows, half)
+        imag = r_in[side, b, 1].reshape(rows, half)
         total = jnp.dot(straight, real, preferred_element_type=F32)
-        total += jnp.dot(turned, imag, preferred_element_type=F32)
-        part[b, 0] = total[:, :half]
-        part[b, 1] = total[:, half:]
-        c_copy(b).start()
+        part[b, side] = total + jnp.dot(l_turn[b], imag, preferred_element_type=F32)
+
+        @pl.when(core != side)
+        def _():
+            c_copy(b).start()
 
     def add_cores(b):
         c_copy(b).wait_recv()
@@ -171,13 +195,13 @@
             f_copy(b, d).start()
         f_in[place, b] = f_out[b, place]
 
-    for step in range(SLOTS + 2):
-        if step < SLOTS:
+    for step in range(len(units) + GAP):
+        if step < len(units):
             multiply(step)
-        if 0 <= step - 1 < SLOTS:
-            add_cores(step - 1)
-        if 0 <= step - 2 < SLOTS:
-            add_teams(step - 2)
+        for lag, work in ((1, add_cores), (GAP, add_teams)):
+            if 0 <= step - lag < len(units):
+                side, b = units[step - lag]
+                pl.when(core == side)(functools.partial(work, b))
     for b in range(SLOTS):
         for d in range(1, GROUP):
             f_copy(b, d).wait_recv()
@@ -192,6 +216,7 @@
         c_copy(b).wait_send()
         for d in range(1, GROUP):
             r_copy(b, d).wait_send()
+            r_copy(b + SLOTS, d).wait_send()
             f_copy(b, d).wait_send()
         for d in range(1, teams):
             z_copy(b, d).wait_send()
@@ -207,23 +232,28 @@
     return pl.pallas_call(
         functools.partial(exchange, n),
         out_shape=jax.ShapeDtypeStruct((GROUP, SLOTS, ROW_TILE, half), BF16),
-        in_specs=[vmem, pl.BlockSpec(memory_space=pl.ANY), vmem, vmem, vmem],
+        in_specs=[pl.BlockSpec(memory_space=pltpu.HBM)] * 5,
         out_specs=vmem,
         scratch_shapes=[
+            pltpu.VMEM(left.shape, BF16),
             pltpu.VMEM(right.shape[1:], BF16),
+            pltpu.VMEM(surf_map.shape, jnp.int32),
+            pltpu.VMEM(shot_map.shape, jnp.int32),
+            pltpu.VMEM(table.shape, BF16),
             pltpu.VMEM((max(teams, receivers // LANES), 2 * BINS * ROW_TILE, LANES), F32),
-            pltpu.VMEM((GROUP, SLOTS, 2, ROW_TILE, receivers), BF16),
+            pltpu.VMEM((2, GROUP, SLOTS, 2, ROW_TILE, half), BF16),
             pltpu.VMEM((n, SLOTS, ROW_TILE, rows), BF16),
-            pltpu.VMEM((SLOTS, 2, GROUP, ROW_TILE, receivers), BF16),
+            pltpu.VMEM((2, SLOTS, 2, GROUP, ROW_TILE, half), BF16),
             pltpu.VMEM((n, SLOTS, ROW_TILE, rows), BF16),
+            pltpu.VMEM((SLOTS, n * ROW_TILE, rows), BF16),
             pltpu.VMEM((SLOTS, 2, n * ROW_TILE, half), F32),
             pltpu.VMEM((SLOTS, n * ROW_TILE, half), F32),
             pltpu.VMEM((SLOTS, teams, rows, half), BF16),
             pltpu.VMEM((SLOTS, teams, rows, half), BF16),
             pltpu.VMEM((SLOTS, GROUP, ROW_TILE, half), BF16),
             pltpu.VMEM((GROUP, SLOTS, ROW_TILE, half), BF16),
-            dma(()),
-            dma((SLOTS, GROUP)), dma((SLOTS, GROUP)),
+            dma((5,)),
+            dma((2 * SLOTS, GROUP)), dma((2 * SLOTS, GROUP)),
             dma((n,)), dma((n,)),
             dma((SLOTS,)), dma((SLOTS,)),
             dma((SLOTS, teams)), dma((SLOTS, teams)),

time: 54.5 us -> 54 us (level)
  the two profiles are of different devices: /device:TPU:0 before, /device:TPU:1 now
where the time goes in v3:
time: 54 us; the launch traced here: 53.7 us
  Pallas kernels  45.8 us (85%)
  local copies, waits for them, and re-layouts  5.95 us (11%)
  matrix products  1.91 us (4%)
    pallas_call x1, Pallas kernels, band_of(): pl.pallas_call(functools.partial(exchange, n), out_shape=jax.ShapeDtypeSt...  45.8 us
    unnamed x14, local copies, waits for them, and re-layouts  5.95 us
    dot_general x2, matrix products, local(): jnp.einsum('csr,ct->srt', band, inverse[part], preferred_element_type=F32)  1.91 us

profile of v3, /device:TPU:1, one launch (start us, length us, event | category | flops | bytes accessed | tf_op | source)
XLA Modules:
  0.0 53.7 jit_solution(9891855899556812450)
XLA Ops:
  0.0 0.0 copy-start
  0.0 2.2 %copy-done = bf16[1,16,512,256]{3,2,1,0:T(8,128)(2,1)S(1)} copy-done((bf16[1,16,512,256]{3,2,1,0:T(8,128)(2,1)S(1)}, bf16[1,16,512,256]{3,2,1,0:T(8,128)(2,1)}, u32[]{:S(2)}) %copy-start) | copy-done | bytes 4194328
  2.2 0.0 copy-start.1
  2.2 1.2 %copy-done.1 = bf16[8,256,256]{2,1,0:T(8,128)(2,1)S(1)} copy-done((bf16[8,256,256]{2,1,0:T(8,128)(2,1)S(1)}, bf16[8,256,256]{2,1,0:T(8,128)(2,1)}, u32[]{:S(2)}) %copy-start.1) | copy-done | bytes 1048600
  3.4 0.0 copy-start.2
  3.4 0.9 %copy-done.2 = bf16[160,256]{1,0:T(8,128)(2,1)S(1)} copy-done((bf16[160,256]{1,0:T(8,128)(2,1)S(1)}, bf16[160,256]{1,0:T(8,128)(2,1)}, u32[]{:S(2)}) %copy-start.2) | copy-done | bytes 81944
  4.3 0.0 copy-start.3
  4.3 0.7 %copy-done.3 = s32[256]{0:T(256)S(1)} copy-done((s32[256]{0:T(256)S(1)}, s32[256]{0:T(256)}, u32[]{:S(2)}) %copy-start.3) | copy-done | bytes 1048
  5.0 0.0 copy-start.4
  5.0 0.7 %copy-done.4 = s32[256]{0:T(256)S(1)} copy-done((s32[256]{0:T(256)S(1)}, s32[256]{0:T(256)}, u32[]{:S(2)}) %copy-start.4) | copy-done | bytes 1048
  5.7 0.0 copy-start.6
  5.7 45.8 %shard_map.73 = bf16[8,5,16,256]{3,2,1,0:T(8,128)(2,1)S(1)} custom-call(bf16[8,256,256]{2,1,0:T(8,128)(2,1)S(1)} %copy-done.1, bf16[1,16,512,256]{3,2,1,0:T(8,128)(2,1)S(1)} %copy-done, s32[1,256]{1,0:T(1,128)S(1)} %bitcast.9, s32[1,256]{1,0:T(1,128)S(1)} %bitcast.10, bf16[160,256]{1,0:T(8,128)(2,1)S(1)} %copy-done.2), custom_call_target="tpu_custom_call" | custom-call | flops 335544320 | bytes 8388608 | tf_op jit(solution)/shard_map/pallas_call | solution.py:232
  51.4 0.0 copy-start.5
  51.4 0.0 copy-done.6
  51.5 0.5 fusion.1
  51.9 0.3 copy-done.5
  52.2 1.4 %add_convert_fusion = bf16[8,256,256]{2,1,0:T(8,128)(2,1)} fusion(f32[8,256,256]{2,1,0:T(8,128)S(1)} %fusion.1, bf16[80,256,1]{1,0,2:T(8,128)(2,1)S(1)} %copy-done.5, bf16[80,8,256]{2,1,0:T(8,128)(2,1)S(1)} %bitcast.8), kind=kOutput, calls=%fused_computation | convolution fusion | flops 84934656 | bytes 3514368 | tf_op jit(solution)/shard_map/csr,ct->srt/dot_general | solution.py:278
Async XLA Ops:
  0.0 2.2 %copy-start = (bf16[1,16,512,256]{3,2,1,0:T(8,128)(2,1)S(1)}, bf16[1,16,512,256]{3,2,1,0:T(8,128)(2,1)}, u32[]{:S(2)}) copy-start(bf16[1,16,512,256]{3,2,1,0:T(8,128)(2,1)} %right_hbm.1) | copy-start | bytes 12582916
  2.2 1.2 %copy-start.1 = (bf16[8,256,256]{2,1,0:T(8,128)(2,1)S(1)}, bf16[8,256,256]{2,1,0:T(8,128)(2,1)}, u32[]{:S(2)}) copy-start(bf16[8,256,256]{2,1,0:T(8,128)(2,1)} %left_hbm.1) | copy-start | bytes 3145732
  3.4 0.9 %copy-start.2 = (bf16[160,256]{1,0:T(8,128)(2,1)S(1)}, bf16[160,256]{1,0:T(8,128)(2,1)}, u32[]{:S(2)}) copy-start(bf16[160,256]{1,0:T(8,128)(2,1)} %constant.6.clone.table_hbm) | copy-start | bytes 245764
  4.3 0.7 %copy-start.3 = (s32[256]{0:T(256)S(1)}, s32[256]{0:T(256)}, u32[]{:S(2)}) copy-start(s32[256]{0:T(256)} %param.9) | copy-start | bytes 3076
  5.0 0.7 %copy-start.4 = (s32[256]{0:T(256)S(1)}, s32[256]{0:T(256)}, u32[]{:S(2)}) copy-start(s32[256]{0:T(256)} %param.10) | copy-start | bytes 3076
  5.7 45.8 %copy-start.6 = (bf16[80,256,1]{1,0,2:T(8,128)(2,1)S(1)}, bf16[80,256,1]{1,0,2:T(8,128)(2,1)}, u32[]{:S(2)}) copy-start(bf16[80,256,1]{1,0,2:T(8,128)(2,1)} %constant.11) | copy-start | bytes 122884
  51.4 0.8 %copy-start.5 = (bf16[80,256,1]{1,0,2:T(8,128)(2,1)S(1)}, bf16[80,256,1]{1,0,2:T(8,128)(2,1)}, u32[]{:S(2)}) copy-start(bf16[80,256,1]{1,0,2:T(8,128)(2,1)} %constant.12) | copy-start | bytes 122884

commit v4 on v3

--- a/solution.py
+++ b/solution.py
@@ -15,9 +15,9 @@
 SLOTS = BINS // GROUP
 ROW_TILE = 16
 LANES = 128
-FIRST = 3
-EARLY = 6
-AHEAD = 4
+FIRST = 2
+EARLY = 4
+AHEAD = 2
 GAP = 3
 F32 = jnp.float32
 BF16 = jnp.bfloat16
@@ -41,7 +41,7 @@
 
 def exchange(n, left_hbm, right_hbm, surf_hbm, shot_hbm, table_hbm, out, left_ref, traces, surf_ref,
              shot_ref, table_ref, lines, right, left,
-             r_in, l_in, l_turn, part, c_in, z_out, z_in, f_out, f_in, fetch_sem,
+             r_in, l_in, l_turn, part, c_out, c_in, z_out, z_in, f_out, f_in, fetch_sem,
              r_send, r_recv, l_send, l_recv, c_send, c_recv, z_send, z_recv, f_send, f_recv):
     teams = n // GROUP
     me = lax.axis_index("src")
@@ -99,8 +99,11 @@
 
     units = [(part_index, b) for part_index in range(2) for b in range(SLOTS)]
 
+    def partner(d):
+        return sum((place // bit % 2 + d // bit % 2) % 2 * bit for bit in (1, 2, 4))
+
     def r_copy(u, d):
-        to = lax.rem(place + d, GROUP)
+        to = partner(d)
         side, b = units[u]
         return pltpu.make_async_remote_copy(
             right.at[side, to, b], r_in.at[side, b, :, place], r_send.at[u, d], r_recv.at[u, d],
@@ -112,7 +115,7 @@
 
     def c_copy(b):
         return pltpu.make_async_remote_copy(
-            part.at[b, other], c_in.at[b], c_send.at[b], c_recv.at[b], device_id={"srf": other})
+            c_out.at[b], c_in.at[b], c_send.at[b], c_recv.at[b], device_id={"srf": other})
 
     def z_copy(b, d):
         to = lax.rem(team + d, teams)
@@ -121,7 +124,7 @@
             device_id={"src": to * GROUP + place})
 
     def f_copy(b, d):
-        to = lax.rem(place + d, GROUP)
+        to = partner(d)
         return pltpu.make_async_remote_copy(
             f_out.at[b, to], f_in.at[place, b], f_send.at[b, d], f_recv.at[b, d],
             device_id={"src": team * GROUP + to})
@@ -175,11 +178,12 @@
 
         @pl.when(core != side)
         def _():
+            c_out[b] = part[b, side].astype(BF16)
             c_copy(b).start()
 
     def add_cores(b):
         c_copy(b).wait_recv()
-        total = part[b, core] + c_in[b]
+        total = part[b, core] + c_in[b].astype(F32)
         part[b, core] = total
         z_out[b] = total.astype(BF16).reshape(teams, rows, half)
         for d in range(1, teams):
@@ -247,7 +251,8 @@
             pltpu.VMEM((n, SLOTS, ROW_TILE, rows), BF16),
             pltpu.VMEM((SLOTS, n * ROW_TILE, rows), BF16),
             pltpu.VMEM((SLOTS, 2, n * ROW_TILE, half), F32),
-            pltpu.VMEM((SLOTS, n * ROW_TILE, half), F32),
+            pltpu.VMEM((SLOTS, n * ROW_TILE, half), BF16),
+            pltpu.VMEM((SLOTS, n * ROW_TILE, half), BF16),
             pltpu.VMEM((SLOTS, teams, rows, half), BF16),
             pltpu.VMEM((SLOTS, teams, rows, half), BF16),
             pltpu.VMEM((SLOTS, GROUP, ROW_TILE, half), BF16),

time: 54 us -> 56 us (1.037)
  Pallas kernels: 45.8 us -> 47.8 us
    pallas_call x1, Pallas kernels: 45.8 us -> 47.8 us  [band_of(): pl.pallas_call(functools.partial(exchange, n), out_shape=jax.ShapeDtypeSt...]
where the time goes in v4:
time: 56 us; the launch traced here: 55.7 us
  Pallas kernels  47.8 us (85%)
  local copies, waits for them, and re-layouts  5.94 us (11%)
  matrix products  1.92 us (3%)
    pallas_call x1, Pallas kernels, band_of(): pl.pallas_call(functools.partial(exchange, n), out_shape=jax.ShapeDtypeSt...  47.8 us
    unnamed x14, local copies, waits for them, and re-layouts  5.94 us
    dot_general x2, matrix products, local(): jnp.einsum('csr,ct->srt', band, inverse[part], preferred_element_type=F32)  1.92 us

profile of v4, /device:TPU:1, one launch (start us, length us, event | category | flops | bytes accessed | tf_op | source)
XLA Modules:
  0.0 55.7 jit_solution(8916591271763800743)
XLA Ops:
  0.0 0.0 copy-start
  0.0 2.2 %copy-done = bf16[1,16,512,256]{3,2,1,0:T(8,128)(2,1)S(1)} copy-done((bf16[1,16,512,256]{3,2,1,0:T(8,128)(2,1)S(1)}, bf16[1,16,512,256]{3,2,1,0:T(8,128)(2,1)}, u32[]{:S(2)}) %copy-start) | copy-done | bytes 4194328
  2.2 0.0 copy-start.1
  2.2 1.2 %copy-done.1 = bf16[8,256,256]{2,1,0:T(8,128)(2,1)S(1)} copy-done((bf16[8,256,256]{2,1,0:T(8,128)(2,1)S(1)}, bf16[8,256,256]{2,1,0:T(8,128)(2,1)}, u32[]{:S(2)}) %copy-start.1) | copy-done | bytes 1048600
  3.4 0.0 copy-start.2
  3.4 0.9 %copy-done.2 = bf16[160,256]{1,0:T(8,128)(2,1)S(1)} copy-done((bf16[160,256]{1,0:T(8,128)(2,1)S(1)}, bf16[160,256]{1,0:T(8,128)(2,1)}, u32[]{:S(2)}) %copy-start.2) | copy-done | bytes 81944
  4.3 0.0 copy-start.3
  4.3 0.7 %copy-done.3 = s32[256]{0:T(256)S(1)} copy-done((s32[256]{0:T(256)S(1)}, s32[256]{0:T(256)}, u32[]{:S(2)}) %copy-start.3) | copy-done | bytes 1048
  5.0 0.0 copy-start.4
  5.0 0.7 %copy-done.4 = s32[256]{0:T(256)S(1)} copy-done((s32[256]{0:T(256)S(1)}, s32[256]{0:T(256)}, u32[]{:S(2)}) %copy-start.4) | copy-done | bytes 1048
  5.7 0.0 copy-start.6
  5.7 47.8 %shard_map.73 = bf16[8,5,16,256]{3,2,1,0:T(8,128)(2,1)S(1)} custom-call(bf16[8,256,256]{2,1,0:T(8,128)(2,1)S(1)} %copy-done.1, bf16[1,16,512,256]{3,2,1,0:T(8,128)(2,1)S(1)} %copy-done, s32[1,256]{1,0:T(1,128)S(1)} %bitcast.9, s32[1,256]{1,0:T(1,128)S(1)} %bitcast.10, bf16[160,256]{1,0:T(8,128)(2,1)S(1)} %copy-done.2), custom_call_target="tpu_custom_call" | custom-call | flops 335544320 | bytes 8388608 | tf_op jit(solution)/shard_map/pallas_call | solution.py:236
  53.5 0.0 copy-start.5
  53.5 0.0 copy-done.6
  53.5 0.5 fusion.1
  54.0 0.3 copy-done.5
  54.3 1.4 %add_convert_fusion = bf16[8,256,256]{2,1,0:T(8,128)(2,1)} fusion(f32[8,256,256]{2,1,0:T(8,128)S(1)} %fusion.1, bf16[80,256,1]{1,0,2:T(8,128)(2,1)S(1)} %copy-done.5, bf16[80,8,256]{2,1,0:T(8,128)(2,1)S(1)} %bitcast.8), kind=kOutput, calls=%fused_computation | convolution fusion | flops 84934656 | bytes 3514368 | tf_op jit(solution)/shard_map/csr,ct->srt/dot_general | solution.py:283
Async XLA Ops:
  0.0 2.2 %copy-start = (bf16[1,16,512,256]{3,2,1,0:T(8,128)(2,1)S(1)}, bf16[1,16,512,256]{3,2,1,0:T(8,128)(2,1)}, u32[]{:S(2)}) copy-start(bf16[1,16,512,256]{3,2,1,0:T(8,128)(2,1)} %right_hbm.1) | copy-start | bytes 12582916
  2.2 1.2 %copy-start.1 = (bf16[8,256,256]{2,1,0:T(8,128)(2,1)S(1)}, bf16[8,256,256]{2,1,0:T(8,128)(2,1)}, u32[]{:S(2)}) copy-start(bf16[8,256,256]{2,1,0:T(8,128)(2,1)} %left_hbm.1) | copy-start | bytes 3145732
  3.4 0.9 %copy-start.2 = (bf16[160,256]{1,0:T(8,128)(2,1)S(1)}, bf16[160,256]{1,0:T(8,128)(2,1)}, u32[]{:S(2)}) copy-start(bf16[160,256]{1,0:T(8,128)(2,1)} %constant.6.clone.table_hbm) | copy-start | bytes 245764
  4.3 0.7 %copy-start.3 = (s32[256]{0:T(256)S(1)}, s32[256]{0:T(256)}, u32[]{:S(2)}) copy-start(s32[256]{0:T(256)} %param.9) | copy-start | bytes 3076
  5.0 0.7 %copy-start.4 = (s32[256]{0:T(256)S(1)}, s32[256]{0:T(256)}, u32[]{:S(2)}) copy-start(s32[256]{0:T(256)} %param.10) | copy-start | bytes 3076
  5.7 47.9 %copy-start.6 = (bf16[80,256,1]{1,0,2:T(8,128)(2,1)S(1)}, bf16[80,256,1]{1,0,2:T(8,128)(2,1)}, u32[]{:S(2)}) copy-start(bf16[80,256,1]{1,0,2:T(8,128)(2,1)} %constant.11) | copy-start | bytes 122884
  53.5 0.8 %copy-start.5 = (bf16[80,256,1]{1,0,2:T(8,128)(2,1)S(1)}, bf16[80,256,1]{1,0,2:T(8,128)(2,1)}, u32[]{:S(2)}) copy-start(bf16[80,256,1]{1,0,2:T(8,128)(2,1)} %constant.12) | copy-start | bytes 122884

commit v5 on v3

--- a/solution.py
+++ b/solution.py
@@ -99,8 +99,11 @@
 
     units = [(part_index, b) for part_index in range(2) for b in range(SLOTS)]
 
+    def partner(d):
+        return sum((place // bit % 2 + d // bit % 2) % 2 * bit for bit in (1, 2, 4))
+
     def r_copy(u, d):
-        to = lax.rem(place + d, GROUP)
+        to = partner(d)
         side, b = units[u]
         return pltpu.make_async_remote_copy(
             right.at[side, to, b], r_in.at[side, b, :, place], r_send.at[u, d], r_recv.at[u, d],
@@ -121,7 +124,7 @@
             device_id={"src": to * GROUP + place})
 
     def f_copy(b, d):
-        to = lax.rem(place + d, GROUP)
+        to = partner(d)
         return pltpu.make_async_remote_copy(
             f_out.at[b, to], f_in.at[place, b], f_send.at[b, d], f_recv.at[b, d],
             device_id={"src": team * GROUP + to})

time: 54 us -> 53.6 us (level)
  no operation moved by 1% of the time
where the time goes in v5:
time: 53.6 us; the launch traced here: 53.3 us
  Pallas kernels  45.4 us (85%)
  local copies, waits for them, and re-layouts  5.95 us (11%)
  matrix products  1.91 us (4%)
    pallas_call x1, Pallas kernels, band_of(): pl.pallas_call(functools.partial(exchange, n), out_shape=jax.ShapeDtypeSt...  45.4 us
    unnamed x14, local copies, waits for them, and re-layouts  5.95 us
    dot_general x2, matrix products, local(): jnp.einsum('csr,ct->srt', band, inverse[part], preferred_element_type=F32)  1.91 us

profile of v5, /device:TPU:1, one launch (start us, length us, event | category | flops | bytes accessed | tf_op | source)
XLA Modules:
  0.0 53.3 jit_solution(12932361001724326579)
XLA Ops:
  0.0 0.0 copy-start
  0.0 2.2 %copy-done = bf16[1,16,512,256]{3,2,1,0:T(8,128)(2,1)S(1)} copy-done((bf16[1,16,512,256]{3,2,1,0:T(8,128)(2,1)S(1)}, bf16[1,16,512,256]{3,2,1,0:T(8,128)(2,1)}, u32[]{:S(2)}) %copy-start) | copy-done | bytes 4194328
  2.2 0.0 copy-start.1
  2.2 1.2 %copy-done.1 = bf16[8,256,256]{2,1,0:T(8,128)(2,1)S(1)} copy-done((bf16[8,256,256]{2,1,0:T(8,128)(2,1)S(1)}, bf16[8,256,256]{2,1,0:T(8,128)(2,1)}, u32[]{:S(2)}) %copy-start.1) | copy-done | bytes 1048600
  3.4 0.0 copy-start.2
  3.4 0.9 %copy-done.2 = bf16[160,256]{1,0:T(8,128)(2,1)S(1)} copy-done((bf16[160,256]{1,0:T(8,128)(2,1)S(1)}, bf16[160,256]{1,0:T(8,128)(2,1)}, u32[]{:S(2)}) %copy-start.2) | copy-done | bytes 81944
  4.3 0.0 copy-start.3
  4.3 0.7 %copy-done.3 = s32[256]{0:T(256)S(1)} copy-done((s32[256]{0:T(256)S(1)}, s32[256]{0:T(256)}, u32[]{:S(2)}) %copy-start.3) | copy-done | bytes 1048
  5.0 0.0 copy-start.4
  5.0 0.7 %copy-done.4 = s32[256]{0:T(256)S(1)} copy-done((s32[256]{0:T(256)S(1)}, s32[256]{0:T(256)}, u32[]{:S(2)}) %copy-start.4) | copy-done | bytes 1048
  5.7 0.0 copy-start.6
  5.7 45.4 %shard_map.73 = bf16[8,5,16,256]{3,2,1,0:T(8,128)(2,1)S(1)} custom-call(bf16[8,256,256]{2,1,0:T(8,128)(2,1)S(1)} %copy-done.1, bf16[1,16,512,256]{3,2,1,0:T(8,128)(2,1)S(1)} %copy-done, s32[1,256]{1,0:T(1,128)S(1)} %bitcast.9, s32[1,256]{1,0:T(1,128)S(1)} %bitcast.10, bf16[160,256]{1,0:T(8,128)(2,1)S(1)} %copy-done.2), custom_call_target="tpu_custom_call" | custom-call | flops 335544320 | bytes 8388608 | tf_op jit(solution)/shard_map/pallas_call | solution.py:235
  51.1 0.0 copy-start.5
  51.1 0.0 copy-done.6
  51.1 0.5 fusion.1
  51.6 0.3 copy-done.5
  51.9 1.4 %add_convert_fusion = bf16[8,256,256]{2,1,0:T(8,128)(2,1)} fusion(f32[8,256,256]{2,1,0:T(8,128)S(1)} %fusion.1, bf16[80,256,1]{1,0,2:T(8,128)(2,1)S(1)} %copy-done.5, bf16[80,8,256]{2,1,0:T(8,128)(2,1)S(1)} %bitcast.8), kind=kOutput, calls=%fused_computation | convolution fusion | flops 84934656 | bytes 3514368 | tf_op jit(solution)/shard_map/csr,ct->srt/dot_general | solution.py:281
Async XLA Ops:
  0.0 2.2 %copy-start = (bf16[1,16,512,256]{3,2,1,0:T(8,128)(2,1)S(1)}, bf16[1,16,512,256]{3,2,1,0:T(8,128)(2,1)}, u32[]{:S(2)}) copy-start(bf16[1,16,512,256]{3,2,1,0:T(8,128)(2,1)} %right_hbm.1) | copy-start | bytes 12582916
  2.2 1.2 %copy-start.1 = (bf16[8,256,256]{2,1,0:T(8,128)(2,1)S(1)}, bf16[8,256,256]{2,1,0:T(8,128)(2,1)}, u32[]{:S(2)}) copy-start(bf16[8,256,256]{2,1,0:T(8,128)(2,1)} %left_hbm.1) | copy-start | bytes 3145732
  3.4 0.9 %copy-start.2 = (bf16[160,256]{1,0:T(8,128)(2,1)S(1)}, bf16[160,256]{1,0:T(8,128)(2,1)}, u32[]{:S(2)}) copy-start(bf16[160,256]{1,0:T(8,128)(2,1)} %constant.6.clone.table_hbm) | copy-start | bytes 245764
  4.3 0.7 %copy-start.3 = (s32[256]{0:T(256)S(1)}, s32[256]{0:T(256)}, u32[]{:S(2)}) copy-start(s32[256]{0:T(256)} %param.9) | copy-start | bytes 3076
  5.0 0.7 %copy-start.4 = (s32[256]{0:T(256)S(1)}, s32[256]{0:T(256)}, u32[]{:S(2)}) copy-start(s32[256]{0:T(256)} %param.10) | copy-start | bytes 3076
  5.7 45.4 %copy-start.6 = (bf16[80,256,1]{1,0,2:T(8,128)(2,1)S(1)}, bf16[80,256,1]{1,0,2:T(8,128)(2,1)}, u32[]{:S(2)}) copy-start(bf16[80,256,1]{1,0,2:T(8,128)(2,1)} %constant.11) | copy-start | bytes 122884
  51.1 0.8 %copy-start.5 = (bf16[80,256,1]{1,0,2:T(8,128)(2,1)S(1)}, bf16[80,256,1]{1,0,2:T(8,128)(2,1)}, u32[]{:S(2)}) copy-start(bf16[80,256,1]{1,0,2:T(8,128)(2,1)} %constant.12) | copy-start | bytes 122884
